TPU v7x, 32 devices: a whole 2x2x4 slice. The times are simulated.
32 devices in a mesh: grp: 2 (over y), row: 4 (over x, core), col: 4 (over z).
Axes of the slice: x: 2, y: 2, z: 4, core: 2. Of those that a mesh axis runs over, the one named last changes fastest.
Arguments:
- homolog_representation: bfloat16 [192, 320, 256], P(('grp', 'row'), 'col'), parts along dimension 0, may hold values from -6 to 6
- occupancy_indicator: int32 [192, 320], P(('grp', 'row'), 'col'), parts along dimension 0, may hold values from 0 to 1, as said below
- standardize_scaling: float32 [256], replicated, may hold values from 0.5 to 1.5
- standardize_shift: float32 [256], replicated, may hold values from -3 to 3
- left_projection_matrix: bfloat16 [256, 32], replicated, may hold values from -0.375 to 0.375
- left_projection_shift: float32 [32], replicated, may hold values from -4 to 4
- right_projection_matrix: bfloat16 [256, 32], replicated, may hold values from -0.375 to 0.375
- right_projection_shift: float32 [32], replicated, may hold values from -4 to 4
- final_projection_matrix: bfloat16 [1024, 128], replicated, may hold values from -0.1875 to 0.1875
- final_projection_shift: float32 [128], replicated, may hold values from -3 to 3
Outputs:
- pair_update: bfloat16 [640, 320, 128], P(('grp', 'row'), 'col'), parts along dimension 0
There are 2 independent parts, one for each index of `grp`. A program takes and returns all parts, laid end to end along the dimension named above; an argument that names none is the same for every part. Nothing has to cross between parts.
Inputs may be any that keep to these rules, and one draw needn't show every extreme that they name: `occupancy_indicator`: the last few sequences may be padding, all zeros. Most entries of the other sequences are 1; each residue has its own share of sequences present, from all of them down to about one per thousand; some residues are present in every sequence that is not padding.
All inputs are finite; a program needn't handle non-finite values.
Results may differ from a plain program's by a relative error of at most 0.0053.
Values may be sent and summed in bfloat16 or wider, within the bound.
A program may use at most 64 MiB of HBM per device.

v0:
```python
import jax
import jax.numpy as jnp
from jax import lax
from jax.sharding import PartitionSpec as P


def local(
    homolog_representation,
    occupancy_indicator,
    standardize_scaling,
    standardize_shift,
    left_projection_matrix,
    left_projection_shift,
    right_projection_matrix,
    right_projection_shift,
    final_projection_matrix,
    final_projection_shift,
):
    homolog_slice_extent, position_slice_extent, feature_extent = homolog_representation.shape
    width = left_projection_matrix.shape[1]
    element_number = homolog_representation.astype(jnp.float32)
    center = element_number - jnp.mean(element_number, axis=-1, keepdims=True)
    spread = jnp.mean(center * center, axis=-1, keepdims=True)
    normed = (center * lax.rsqrt(spread + 1e-05) * standardize_scaling + standardize_shift).astype(
        jnp.bfloat16
    )
    weights = jnp.concatenate([left_projection_matrix, right_projection_matrix], axis=1)
    offsets = jnp.concatenate([left_projection_shift, right_projection_shift])
    keep_flags = occupancy_indicator.astype(jnp.float32).reshape(
        homolog_slice_extent * position_slice_extent, 1
    )
    mixed = jnp.dot(
        normed.reshape(homolog_slice_extent * position_slice_extent, feature_extent),
        weights,
        preferred_element_type=jnp.float32,
    )
    mixed = (
        ((mixed + offsets) * keep_flags)
        .astype(jnp.bfloat16)
        .reshape(homolog_slice_extent, position_slice_extent, 2 * width)
    )
    left_loc = mixed[:, :, :width]
    right_loc = mixed[:, :, width:]
    presence_flags = occupancy_indicator.astype(jnp.bfloat16)
    right_slab, col_mask = (
        lax.all_gather(right_loc, "row", axis=0, tiled=True),
        lax.all_gather(presence_flags, "row", axis=0, tiled=True),
    )
    left_wide, mask_wide = (
        lax.all_gather(left_loc, "col", axis=1, tiled=True),
        lax.all_gather(presence_flags, "col", axis=1, tiled=True),
    )
    left_slab, row_mask = (
        lax.all_to_all(left_wide, "row", split_axis=1, concat_axis=0, tiled=True),
        lax.all_to_all(mask_wide, "row", split_axis=1, concat_axis=0, tiled=True),
    )
    homolog_extent = right_slab.shape[0]
    cols = right_slab.shape[1]
    rows = left_slab.shape[1]
    nblk = rows // 8
    left_blocks = jnp.transpose(left_slab.reshape(homolog_extent, nblk, 8 * width), (1, 0, 2))
    mask_blocks = jnp.transpose(row_mask.reshape(homolog_extent, nblk, 8), (1, 0, 2))
    right_flat = right_slab.reshape(homolog_extent, cols * width)
    w_grid = final_projection_matrix.reshape(width, width, -1)

    def tile(pair):
        lblk, mblk = pair
        outer = lax.dot_general(
            lblk, right_flat, (((0,), (0,)), ((), ())), preferred_element_type=jnp.float32
        )
        outer = outer.astype(jnp.bfloat16).reshape(8, width, cols, width)
        proj = (
            jnp.einsum("ipjq,pqo->ijo", outer, w_grid, preferred_element_type=jnp.float32)
            + final_projection_shift
        )
        count = lax.dot_general(
            mblk, col_mask, (((0,), (0,)), ((), ())), preferred_element_type=jnp.float32
        )
        return (proj / jnp.maximum(count, 1.0)[..., None]).astype(jnp.bfloat16)

    tiles = lax.map(tile, (left_blocks, mask_blocks))
    return tiles.reshape(rows, cols, -1)


def solution(mesh):
    placed = (
        P(("grp", "row"), "col", None),
        P(("grp", "row"), "col"),
        P(),
        P(),
        P(),
        P(),
        P(),
        P(),
        P(),
        P(),
    )
    return jax.shard_map(
        local, mesh=mesh, in_specs=placed, out_specs=P(("grp", "row"), "col", None), check_vma=False
    )
```

profile of v0, /device:TPU:1, one launch (start us, length us, event | category | flops | bytes accessed | tf_op | source)
XLA Modules:
  0.0 189.3 jit_solution(17987195917150191011)
XLA Ops:
  0.8 11.3 %all-gather = bf16[4,80,24]{1,2,0:T(8,128)(2,1)S(1)} all-gather(bf16[1,80,24]{1,2,0:T(8,128)(2,1)S(1)} %bitcast.77), channel_id=1, replica_groups=mesh['grp'=2,'row'=4,'col'=4] {'col'}, dimensions={0}, use_global_device_ids=true | all-gather | bytes 19200 | tf_op jit(solution)/shard_map/all_gather | solution.py:51
  13.0 6.8 %all-to-all-start.1 = ((bf16[24,4,80]{2,0,1:T(8,128)(2,1)}), bf16[24,4,80]{2,0,1:T(8,128)(2,1)S(1)}, u32[]{:S(2)}, u32[]{:S(2)}) async-start(bf16[24,4,80]{2,0,1:T(8,128)(2,1)} %copy.34), calls=%async_computation.1 | async-start | bytes 49152 | tf_op jit(solution)/shard_map/all_to_all | solution.py:55
  24.4 35.5 %all_gather.12 = bf16[24,320,32]{2,0,1:T(8,128)(2,1)S(1)} all-gather(bf16[24,80,32]{2,0,1:T(8,128)(2,1)S(1)} %copy.41), channel_id=1, replica_groups=mesh['grp'=2,'row'=4,'col'=4] {'col'}, dimensions={1}, use_global_device_ids=true | all-gather | bytes 614400 | tf_op jit(solution)/shard_map/all_gather | solution.py:50
  66.7 13.4 %all_gather.13 = bf16[96,80,32]{1,2,0:T(8,128)(2,1)S(1)} all-gather(bf16[24,80,32]{1,2,0:T(8,128)(2,1)S(1)} %copy.42), channel_id=1, replica_groups=mesh['grp'=2,'row'=4,'col'=4] {'row'}, dimensions={0}, use_global_device_ids=true | all-gather | bytes 614400 | tf_op jit(solution)/shard_map/all_gather | solution.py:46
  81.8 5.2 %all_gather.15 = bf16[96,80]{1,0:T(8,128)(2,1)S(1)} all-gather(bf16[24,80]{1,0:T(8,128)(2,1)S(1)} %get-tuple-element.90), channel_id=1, replica_groups=mesh['grp'=2,'row'=4,'col'=4] {'row'}, dimensions={0}, use_global_device_ids=true | all-gather | bytes 19200 | tf_op jit(solution)/shard_map/all_gather | solution.py:47
  92.8 96.4 %while.10 = (s32[]{:T(128)}, bf16[10,8,80,128]{3,2,1,0:T(8,128)(2,1)}, bf16[10,96,256]{2,1,0:T(8,128)(2,1)S(1)}, bf16[96,2560]{1,0:T(8,128)(2,1)S(1)}, bf16[32,3...) while((s32[]{:T(128)}, ...), condition=%wide.region_3.4_spmd, body=%wide.region_2.3_spmd.sunk | while | flops 294625920 | bytes 10174565 | solution.py:81
  93.4 4.7 %reshape.62 = bf16[8,32,80,32]{3,2,1,0:T(8,128)(2,1)} reshape(bf16[256,2560]{1,0:T(8,128)(2,1)S(1)} %convolution_convert_fusion.2) | data formatting | bytes 2621440 | tf_op jit(solution)/shard_map/while/body/eval_jaxpr/reshape | solution.py:71
  98.2 4.3 %fusion.43 = bf16[10,8,80,128]{3,2,1,0:T(8,128)(2,1)} fusion(bf16[10,8,80,128]{3,2,1,0:T(8,128)(2,1)} %get-tuple-element.151, s32[]{:T(128)} %get-tuple-element.150, bf16[8,32,80,32]{3,2,1,0:T(8,128)(2,1)} %reshape.62, bf16[32,32,128]{2,1,0:T(8,128)(2,1)S(1)} %get-tuple-element.163, f32[8,80]{1,0:T(8,128)S(1)} %convolution_maximum_fusion.2, ...), kind=kOutput, calls=%fused_computation.6.clone.1 | convolution fusion | flops 168017920 | bytes 5672448 | tf_op jit(solution)/shard_map/while/body/eval_jaxpr/ipjq,pqo->ijo/dot_general | solution.py:73
  103.0 4.7 %reshape.62 = bf16[8,32,80,32]{3,2,1,0:T(8,128)(2,1)} reshape(bf16[256,2560]{1,0:T(8,128)(2,1)S(1)} %convolution_convert_fusion.2) | data formatting | bytes 2621440 | tf_op jit(solution)/shard_map/while/body/eval_jaxpr/reshape | solution.py:71
  107.8 4.3 %fusion.43 = bf16[10,8,80,128]{3,2,1,0:T(8,128)(2,1)} fusion(bf16[10,8,80,128]{3,2,1,0:T(8,128)(2,1)} %get-tuple-element.151, s32[]{:T(128)} %get-tuple-element.150, bf16[8,32,80,32]{3,2,1,0:T(8,128)(2,1)} %reshape.62, bf16[32,32,128]{2,1,0:T(8,128)(2,1)S(1)} %get-tuple-element.163, f32[8,80]{1,0:T(8,128)S(1)} %convolution_maximum_fusion.2, ...), kind=kOutput, calls=%fused_computation.6.clone.1 | convolution fusion | flops 168017920 | bytes 5672448 | tf_op jit(solution)/shard_map/while/body/eval_jaxpr/ipjq,pqo->ijo/dot_general | solution.py:73
  112.7 4.7 %reshape.62 = bf16[8,32,80,32]{3,2,1,0:T(8,128)(2,1)} reshape(bf16[256,2560]{1,0:T(8,128)(2,1)S(1)} %convolution_convert_fusion.2) | data formatting | bytes 2621440 | tf_op jit(solution)/shard_map/while/body/eval_jaxpr/reshape | solution.py:71
  122.3 4.7 %reshape.62 = bf16[8,32,80,32]{3,2,1,0:T(8,128)(2,1)} reshape(bf16[256,2560]{1,0:T(8,128)(2,1)S(1)} %convolution_convert_fusion.2) | data formatting | bytes 2621440 | tf_op jit(solution)/shard_map/while/body/eval_jaxpr/reshape | solution.py:71
  127.1 4.3 %fusion.43 = bf16[10,8,80,128]{3,2,1,0:T(8,128)(2,1)} fusion(bf16[10,8,80,128]{3,2,1,0:T(8,128)(2,1)} %get-tuple-element.151, s32[]{:T(128)} %get-tuple-element.150, bf16[8,32,80,32]{3,2,1,0:T(8,128)(2,1)} %reshape.62, bf16[32,32,128]{2,1,0:T(8,128)(2,1)S(1)} %get-tuple-element.163, f32[8,80]{1,0:T(8,128)S(1)} %convolution_maximum_fusion.2, ...), kind=kOutput, calls=%fused_computation.6.clone.1 | convolution fusion | flops 168017920 | bytes 5672448 | tf_op jit(solution)/shard_map/while/body/eval_jaxpr/ipjq,pqo->ijo/dot_general | solution.py:73
  131.9 4.7 %reshape.62 = bf16[8,32,80,32]{3,2,1,0:T(8,128)(2,1)} reshape(bf16[256,2560]{1,0:T(8,128)(2,1)S(1)} %convolution_convert_fusion.2) | data formatting | bytes 2621440 | tf_op jit(solution)/shard_map/while/body/eval_jaxpr/reshape | solution.py:71
  136.8 4.3 %fusion.43 = bf16[10,8,80,128]{3,2,1,0:T(8,128)(2,1)} fusion(bf16[10,8,80,128]{3,2,1,0:T(8,128)(2,1)} %get-tuple-element.151, s32[]{:T(128)} %get-tuple-element.150, bf16[8,32,80,32]{3,2,1,0:T(8,128)(2,1)} %reshape.62, bf16[32,32,128]{2,1,0:T(8,128)(2,1)S(1)} %get-tuple-element.163, f32[8,80]{1,0:T(8,128)S(1)} %convolution_maximum_fusion.2, ...), kind=kOutput, calls=%fused_computation.6.clone.1 | convolution fusion | flops 168017920 | bytes 5672448 | tf_op jit(solution)/shard_map/while/body/eval_jaxpr/ipjq,pqo->ijo/dot_general | solution.py:73
  141.6 4.7 %reshape.62 = bf16[8,32,80,32]{3,2,1,0:T(8,128)(2,1)} reshape(bf16[256,2560]{1,0:T(8,128)(2,1)S(1)} %convolution_convert_fusion.2) | data formatting | bytes 2621440 | tf_op jit(solution)/shard_map/while/body/eval_jaxpr/reshape | solution.py:71
  146.4 4.3 %fusion.43 = bf16[10,8,80,128]{3,2,1,0:T(8,128)(2,1)} fusion(bf16[10,8,80,128]{3,2,1,0:T(8,128)(2,1)} %get-tuple-element.151, s32[]{:T(128)} %get-tuple-element.150, bf16[8,32,80,32]{3,2,1,0:T(8,128)(2,1)} %reshape.62, bf16[32,32,128]{2,1,0:T(8,128)(2,1)S(1)} %get-tuple-element.163, f32[8,80]{1,0:T(8,128)S(1)} %convolution_maximum_fusion.2, ...), kind=kOutput, calls=%fused_computation.6.clone.1 | convolution fusion | flops 168017920 | bytes 5672448 | tf_op jit(solution)/shard_map/while/body/eval_jaxpr/ipjq,pqo->ijo/dot_general | solution.py:73
  151.2 4.7 %reshape.62 = bf16[8,32,80,32]{3,2,1,0:T(8,128)(2,1)} reshape(bf16[256,2560]{1,0:T(8,128)(2,1)S(1)} %convolution_convert_fusion.2) | data formatting | bytes 2621440 | tf_op jit(solution)/shard_map/while/body/eval_jaxpr/reshape | solution.py:71
  160.9 4.7 %reshape.62 = bf16[8,32,80,32]{3,2,1,0:T(8,128)(2,1)} reshape(bf16[256,2560]{1,0:T(8,128)(2,1)S(1)} %convolution_convert_fusion.2) | data formatting | bytes 2621440 | tf_op jit(solution)/shard_map/while/body/eval_jaxpr/reshape | solution.py:71
  165.7 4.3 %fusion.43 = bf16[10,8,80,128]{3,2,1,0:T(8,128)(2,1)} fusion(bf16[10,8,80,128]{3,2,1,0:T(8,128)(2,1)} %get-tuple-element.151, s32[]{:T(128)} %get-tuple-element.150, bf16[8,32,80,32]{3,2,1,0:T(8,128)(2,1)} %reshape.62, bf16[32,32,128]{2,1,0:T(8,128)(2,1)S(1)} %get-tuple-element.163, f32[8,80]{1,0:T(8,128)S(1)} %convolution_maximum_fusion.2, ...), kind=kOutput, calls=%fused_computation.6.clone.1 | convolution fusion | flops 168017920 | bytes 5672448 | tf_op jit(solution)/shard_map/while/body/eval_jaxpr/ipjq,pqo->ijo/dot_general | solution.py:73
  170.5 4.7 %reshape.62 = bf16[8,32,80,32]{3,2,1,0:T(8,128)(2,1)} reshape(bf16[256,2560]{1,0:T(8,128)(2,1)S(1)} %convolution_convert_fusion.2) | data formatting | bytes 2621440 | tf_op jit(solution)/shard_map/while/body/eval_jaxpr/reshape | solution.py:71
  175.3 4.3 %fusion.43 = bf16[10,8,80,128]{3,2,1,0:T(8,128)(2,1)} fusion(bf16[10,8,80,128]{3,2,1,0:T(8,128)(2,1)} %get-tuple-element.151, s32[]{:T(128)} %get-tuple-element.150, bf16[8,32,80,32]{3,2,1,0:T(8,128)(2,1)} %reshape.62, bf16[32,32,128]{2,1,0:T(8,128)(2,1)S(1)} %get-tuple-element.163, f32[8,80]{1,0:T(8,128)S(1)} %convolution_maximum_fusion.2, ...), kind=kOutput, calls=%fused_computation.6.clone.1 | convolution fusion | flops 168017920 | bytes 5672448 | tf_op jit(solution)/shard_map/while/body/eval_jaxpr/ipjq,pqo->ijo/dot_general | solution.py:73
  180.2 4.7 %reshape.62 = bf16[8,32,80,32]{3,2,1,0:T(8,128)(2,1)} reshape(bf16[256,2560]{1,0:T(8,128)(2,1)S(1)} %convolution_convert_fusion.2) | data formatting | bytes 2621440 | tf_op jit(solution)/shard_map/while/body/eval_jaxpr/reshape | solution.py:71
  185.0 4.3 %fusion.43 = bf16[10,8,80,128]{3,2,1,0:T(8,128)(2,1)} fusion(bf16[10,8,80,128]{3,2,1,0:T(8,128)(2,1)} %get-tuple-element.151, s32[]{:T(128)} %get-tuple-element.150, bf16[8,32,80,32]{3,2,1,0:T(8,128)(2,1)} %reshape.62, bf16[32,32,128]{2,1,0:T(8,128)(2,1)S(1)} %get-tuple-element.163, f32[8,80]{1,0:T(8,128)S(1)} %convolution_maximum_fusion.2, ...), kind=kOutput, calls=%fused_computation.6.clone.1 | convolution fusion | flops 168017920 | bytes 5672448 | tf_op jit(solution)/shard_map/while/body/eval_jaxpr/ipjq,pqo->ijo/dot_general | solution.py:73
  (71 shorter events, 35.6 us)
Async XLA Ops:
  0.0 21.4 %copy-start = (bf16[24,80,256]{2,1,0:T(8,128)(2,1)S(1)}, bf16[24,80,256]{2,1,0:T(8,128)(2,1)}, u32[]{:S(2)}) copy-start(bf16[24,80,256]{2,1,0:T(8,128)(2,1)} %param.12) | copy-start | bytes 2949124
  0.0 22.3 %copy-start.7 = (f32[32]{0:T(128)S(1)}, f32[32]{0:T(128)}, u32[]{:S(2)}) copy-start(f32[32]{0:T(128)} %param.17) | copy-start | bytes 388
  0.0 22.3 %copy-start.6 = (f32[32]{0:T(128)S(1)}, f32[32]{0:T(128)}, u32[]{:S(2)}) copy-start(f32[32]{0:T(128)} %param.19) | copy-start | bytes 388
  0.0 22.4 %copy-start.4 = (f32[256]{0:T(256)S(1)}, f32[256]{0:T(256)}, u32[]{:S(2)}) copy-start(f32[256]{0:T(256)} %param.14) | copy-start | bytes 3076
  0.0 22.4 %copy-start.3 = (f32[256]{0:T(256)S(1)}, f32[256]{0:T(256)}, u32[]{:S(2)}) copy-start(f32[256]{0:T(256)} %param.15) | copy-start | bytes 3076
  13.0 49.5 %all-to-all-start.1 = ((bf16[24,4,80]{2,0,1:T(8,128)(2,1)}), bf16[24,4,80]{2,0,1:T(8,128)(2,1)S(1)}, u32[]{:S(2)}, u32[]{:S(2)}) async-start(bf16[24,4,80]{2,0,1:T(8,128)(2,1)} %copy.34), calls=%async_computation.1 | async-start | bytes 49152 | tf_op jit(solution)/shard_map/all_to_all | solution.py:55
  19.7 3.4 %copy-start.1 = (bf16[256,32]{0,1:T(8,128)(2,1)S(1)}, bf16[256,32]{0,1:T(8,128)(2,1)}, u32[]{:S(2)}) copy-start(bf16[256,32]{0,1:T(8,128)(2,1)} %param.18) | copy-start | bytes 49156
  19.7 3.4 %copy-start.2 = (bf16[256,32]{0,1:T(8,128)(2,1)S(1)}, bf16[256,32]{0,1:T(8,128)(2,1)}, u32[]{:S(2)}) copy-start(bf16[256,32]{0,1:T(8,128)(2,1)} %param.16) | copy-start | bytes 49156
  62.4 24.8 %all-to-all-start = ((bf16[4,2,30720]{2,1,0:T(2,128)(2,1)}), bf16[4,2,30720]{2,1,0:T(2,128)(2,1)S(1)}, u32[]{:S(2)}, u32[]{:S(2)}) async-start(bf16[4,2,30720]{2,1,0:T(2,128)(2,1)} %reshape.59), calls=%async_computation | async-start | bytes 983040 | tf_op jit(solution)/shard_map/all_to_all | solution.py:54
  91.1 1.7 copy-start.5
  91.1 1.7 copy-start.8
where the time goes:
time: 190 us; the launch traced here: 189 us
  blocking collectives  65.3 us (34%)
  local copies, waits for them, and re-layouts  58.8 us (31%)
  matrix products  49.8 us (26%)
  starting transfers between devices  11 us (6%)
  other arithmetic  4.05 us (2%)
    reshape x10, local copies, waits for them, and re-layouts, tile(): outer = outer.astype(jnp.bfloat16).reshape(8, width, cols, width)  47 us
    dot_general x10, matrix products, tile(): jnp.einsum('ipjq,pqo->ijo', outer, w_grid, preferred_element_type=jnp.flo...  42.9 us
    all_gather x1, blocking collectives, local(): lax.all_gather(left_loc, 'col', axis=1, tiled=True)  35.5 us
    all_gather x1, blocking collectives, local(): lax.all_gather(right_loc, 'row', axis=0, tiled=True)  13.4 us
    all_gather x1, blocking collectives, local(): lax.all_gather(presence_flags, 'col', axis=1, tiled=True)  11.3 us
    all_to_all x1, starting transfers between devices, local(): lax.all_to_all(mask_wide, 'row', split_axis=1, concat_axis=0, tiled=True)  6.76 us
    dot_general x10, matrix products, tile(): lax.dot_general(lblk, right_flat, (((0,), (0,)), ((), ())), preferred_ele...  5.24 us
    all_gather x1, blocking collectives, local(): lax.all_gather(presence_flags, 'row', axis=0, tiled=True)  5.16 us
  transfers between devices with their start and end apart: 2, of which 0 were waited for; matrix products, arithmetic and copies ran while one was open for 5% of the time, Pallas kernels for 0%

commit v1 on v0

v1 whole, which is shorter than its diff:
```python
import functools

import jax
import jax.numpy as jnp
from jax import lax
from jax.experimental import pallas as pl
from jax.experimental.pallas import tpu as pltpu
from jax.sharding import PartitionSpec as P

MESH = pl.DeviceIdType.MESH
LANES = 128
VMEM_LIMIT = 56 * 1024 * 1024


def exchange_kernel(
    n,
    x_ref,
    gain_ref,
    bias_ref,
    wl_ref,
    bl_ref,
    wr_ref,
    br_ref,
    flat_sj_ref,
    flat_is_ref,
    mask_ref,
    lg_ref,
    rg_ref,
    ml_ref,
    mr_ref,
    norm_sj,
    norm_is,
    left_own,
    l_send,
    l_recv,
    r_send,
    r_recv,
    ml_send,
    ml_recv,
    mr_send,
    mr_recv,
):
    seqs, res, feat = x_ref.shape
    halves = feat // LANES
    tokens = seqs * res
    grp = lax.axis_index("grp")
    row = lax.axis_index("row")
    col = lax.axis_index("col")
    own = row == col

    barrier = pltpu.get_barrier_semaphore()
    for d in range(1, n):
        pl.semaphore_signal(barrier, inc=1, device_id=(grp, lax.rem(row + d, n), col), device_id_type=MESH)
        pl.semaphore_signal(barrier, inc=1, device_id=(grp, lax.rem(row + d, n), row), device_id_type=MESH)

    @pl.when(jnp.logical_not(own))
    def _():
        pl.semaphore_signal(barrier, inc=1, device_id=(grp, row, row), device_id_type=MESH)

    gain = gain_ref[...]
    bias = bias_ref[...]

    def normalize(s, carry):
        e = x_ref[s].astype(jnp.float32)
        center = e - jnp.mean(e, axis=-1, keepdims=True)
        spread = jnp.mean(center * center, axis=-1, keepdims=True)
        v = center * lax.rsqrt(spread + 1e-05) * gain + bias
        at = pl.multiple_of(s * res, 8)
        for h in range(halves):
            norm_sj[h, pl.ds(at, res), :] = v[:, h * LANES : (h + 1) * LANES]
        return carry

    lax.fori_loop(0, seqs, normalize, 0)

    def reorder(i, carry):
        at = pl.multiple_of(i * seqs, 8)
        for h in range(halves):
            norm_is[h, pl.ds(at, seqs), :] = norm_sj[h, pl.ds(i, seqs, stride=res), :]
        return carry

    lax.fori_loop(0, res, reorder, 0, unroll=4)

    def project(src, w_ref, b_ref, flat_ref):
        total = b_ref[...]
        acc = None
        for h in range(halves):
            part = lax.dot_general(
                w_ref[:, h * LANES : (h + 1) * LANES],
                src[h].astype(jnp.bfloat16),
                (((1,), (1,)), ((), ())),
                preferred_element_type=jnp.float32,
            )
            acc = part if acc is None else acc + part
        return ((acc + total) * flat_ref[...]).astype(jnp.bfloat16)

    left_own[...] = project(norm_is, wl_ref, bl_ref, flat_is_ref)

    others = (n - 1) + n - own.astype(jnp.int32)
    pl.semaphore_wait(barrier, others)

    def left_copies(d):
        target = (grp, col, lax.rem(col + d, n))
        return (
            pltpu.make_async_remote_copy(
                src_ref=left_own, dst_ref=lg_ref.at[row], send_sem=l_send.at[d], recv_sem=l_recv.at[row],
                device_id=target, device_id_type=MESH,
            ),
            pltpu.make_async_remote_copy(
                src_ref=mask_ref, dst_ref=ml_ref.at[row], send_sem=ml_send.at[d], recv_sem=ml_recv.at[row],
                device_id=target, device_id_type=MESH,
            ),
        )

    def right_copies(d):
        target = (grp, lax.rem(row + d, n), col)
        return (
            pltpu.make_async_remote_copy(
                src_ref=rg_ref.at[row], dst_ref=rg_ref.at[row], send_sem=r_send.at[d], recv_sem=r_recv.at[row],
                device_id=target, device_id_type=MESH,
            ),
            pltpu.make_async_remote_copy(
                src_ref=mask_ref, dst_ref=mr_ref.at[row], send_sem=mr_send.at[d], recv_sem=mr_recv.at[row],
                device_id=target, device_id_type=MESH,
            ),
        )

    for d in range(1, n):
        for copy in left_copies(d):
            copy.start()

    @pl.when(jnp.logical_not(own))
    def _():
        for copy in left_copies(0):
            copy.start()

    rg_ref[row] = project(norm_sj, wr_ref, br_ref, flat_sj_ref)
    for d in range(1, n):
        for copy in right_copies(d):
            copy.start()

    mr_ref[row] = mask_ref[...]

    @pl.when(own)
    def _():
        lg_ref[row] = left_own[...]
        ml_ref[row] = mask_ref[...]

    for d in range(1, n):
        for copy in left_copies(d) + right_copies(d):
            copy.wait_send()

    @pl.when(jnp.logical_not(own))
    def _():
        for copy in left_copies(0):
            copy.wait_send()

    def arrived(dst, slot, sem):
        pltpu.make_async_remote_copy(
            src_ref=dst.at[slot], dst_ref=dst.at[slot], send_sem=l_send.at[0], recv_sem=sem.at[slot],
            device_id=(grp, lax.rem(row + 1, n), col), device_id_type=MESH,
        ).wait_recv()

    for d in range(1, n):
        slot = lax.rem(row + d, n)
        arrived(rg_ref, slot, r_recv)
        arrived(mr_ref, slot, mr_recv)
        arrived(lg_ref, slot, l_recv)
        arrived(ml_ref, slot, ml_recv)

    @pl.when(jnp.logical_not(own))
    def _():
        arrived(lg_ref, row, l_recv)
        arrived(ml_ref, row, ml_recv)


def pair_kernel(
    seqs, res, lg_ref, rg_ref, ml_ref, mr_ref, wt_ref, shift_ref, out_ref, stage, right, left, outer, scale
):
    n, width, _ = rg_ref.shape
    block = out_ref.shape[0]
    step = pl.program_id(0)

    @pl.when(step == 0)
    def _():
        blank = jnp.zeros((width, LANES - res), jnp.float32)
        for k in range(n):
            for s in range(seqs):
                piece = rg_ref[k, :, s * res : (s + 1) * res].astype(jnp.float32)
                at = (k * seqs + s) * width
                stage[at : at + width, :] = jnp.concatenate([piece, blank], axis=1)
        for q in range(width):
            right[:, q * LANES : (q + 1) * LANES] = stage[pl.ds(q, n * seqs, stride=width), :].astype(
                jnp.bfloat16
            )
        count = lax.dot_general(
            ml_ref[...].reshape(n * seqs, LANES).astype(jnp.bfloat16),
            mr_ref[...].reshape(n * seqs, LANES).astype(jnp.bfloat16),
            (((0,), (0,)), ((), ())),
            preferred_element_type=jnp.float32,
        )
        scale[...] = 1.0 / jnp.maximum(count, 1.0)

    for i in range(block):
        left[i * width : (i + 1) * width, :] = jnp.concatenate(
            [lg_ref[k, :, i * seqs : (i + 1) * seqs] for k in range(n)], axis=1
        )

    wide = 2 * LANES

    def products(c, carry):
        at = pl.multiple_of(c * wide, wide)
        acc = jnp.dot(left[...], right[:, pl.ds(at, wide)], preferred_element_type=jnp.float32).astype(
            jnp.bfloat16
        )
        for h in range(2):
            low = pl.multiple_of((2 * c + h) * width, width)
            for i in range(block):
                outer[pl.ds(low, width), i * LANES : (i + 1) * LANES] = acc[
                    i * width : (i + 1) * width, h * LANES : (h + 1) * LANES
                ]
        return carry

    lax.fori_loop(0, width // 2, products, 0, unroll=2)

    shift = shift_ref[...]
    for c in range(block // 2):
        acc = jnp.dot(wt_ref[...], outer[:, c * wide : (c + 1) * wide], preferred_element_type=jnp.float32)
        for h in range(2):
            i = 2 * c + h
            one = (acc[:, h * LANES : (h + 1) * LANES] + shift) * scale[pl.ds(step * block + i, 1), :]
            out_ref[i] = one.T[:res].astype(jnp.bfloat16)


def local(n, x, occupancy, gain, bias, wl, bl, wr, br, wf, bf):
    seqs, res, feat = x.shape
    width = wl.shape[1]
    pair = wf.shape[1]
    tokens = seqs * res
    occ = occupancy.astype(jnp.float32)
    flat_sj = occ.reshape(1, tokens)
    flat_is = occ.T.reshape(1, tokens)
    mask = jnp.pad(occ, ((0, 0), (0, LANES - res)))
    whole = pl.BlockSpec(memory_space=pltpu.VMEM)
    dma = pltpu.SemaphoreType.DMA((n,))
    lg, rg, ml, mr = pl.pallas_call(
        functools.partial(exchange_kernel, n),
        out_shape=(
            jax.ShapeDtypeStruct((n, width, tokens), jnp.bfloat16),
            jax.ShapeDtypeStruct((n, width, tokens), jnp.bfloat16),
            jax.ShapeDtypeStruct((n, seqs, LANES), jnp.float32),
            jax.ShapeDtypeStruct((n, seqs, LANES), jnp.float32),
        ),
        in_specs=[whole] * 10,
        out_specs=(whole,) * 4,
        scratch_shapes=[
            pltpu.VMEM((feat // LANES, tokens, LANES), jnp.float32),
            pltpu.VMEM((feat // LANES, tokens, LANES), jnp.float32),
            pltpu.VMEM((width, tokens), jnp.bfloat16),
        ]
        + [dma] * 8,
        compiler_params=pltpu.CompilerParams(
            collective_id=0, has_side_effects=True, vmem_limit_bytes=VMEM_LIMIT
        ),
    )(
        x,
        gain.reshape(1, feat),
        bias.reshape(1, feat),
        wl.T,
        bl.reshape(width, 1),
        wr.T,
        br.reshape(width, 1),
        flat_sj,
        flat_is,
        mask,
    )
    wt = jnp.transpose(wf.reshape(width, width, pair), (2, 1, 0)).reshape(pair, width * width)
    block = 16
    depth = n * seqs

    def fixed(*shape):
        return pl.BlockSpec(shape, lambda b: (0,) * len(shape))

    return pl.pallas_call(
        functools.partial(pair_kernel, seqs, res),
        grid=(res // block,),
        out_shape=jax.ShapeDtypeStruct((res, res, pair), jnp.bfloat16),
        in_specs=[
            pl.BlockSpec((n, width, block * seqs), lambda b: (0, 0, b)),
            fixed(n, width, tokens),
            fixed(n, seqs, LANES),
            fixed(n, seqs, LANES),
            fixed(pair, width * width),
            fixed(pair, 1),
        ],
        out_specs=pl.BlockSpec((block, res, pair), lambda b: (b, 0, 0)),
        scratch_shapes=[
            pltpu.VMEM((depth * width, LANES), jnp.float32),
            pltpu.VMEM((depth, width * LANES), jnp.bfloat16),
            pltpu.VMEM((block * width, depth), jnp.bfloat16),
            pltpu.VMEM((width * width, block * LANES), jnp.bfloat16),
            pltpu.VMEM((LANES, LANES), jnp.float32),
        ],
        compiler_params=pltpu.CompilerParams(vmem_limit_bytes=VMEM_LIMIT),
    )(lg, rg, ml, mr, wt, bf.reshape(pair, 1))


def solution(mesh):
    placed = (P(("grp", "row"), "col", None), P(("grp", "row"), "col")) + (P(),) * 8
    return jax.shard_map(
        functools.partial(local, mesh.shape["row"]),
        mesh=mesh,
        in_specs=placed,
        out_specs=P(("grp", "row"), "col", None),
        check_vma=False,
    )
```

time: 190 us -> 52.9 us (0.28)
  blocking collectives: 65.3 us -> 0 us
  local copies, waits for them, and re-layouts: 58.8 us -> 8.03 us
  matrix products: 49.8 us -> 0 us
  Pallas kernels: 0 us -> 43.9 us
  starting transfers between devices: 11 us -> 0 us
  other arithmetic: 4.05 us -> 0.71 us
    all_gather x4 -> x0, blocking collectives: 65.3 us -> none  [the longest x1 35.5 us: local(): lax.all_gather(left_loc, 'col', axis=1, tiled=True)]
    dot_general x31 -> x0, matrix products: 49.8 us -> none  [the longest x10 42.9 us: tile(): jnp.einsum('ipjq,pqo->ijo', outer, w_grid, preferred_element_type=jnp.flo...]
    pallas_call x0 -> x2, Pallas kernels: none -> 43.9 us  [the longest x1 22.7 us: local(): pl.pallas_call(functools.partial(exchange_kernel, n), out_shape=(jax.Shap...]
    reshape x13 -> x6, local copies, waits for them, and re-layouts: 49.1 us -> 6.29 us  [the longest x1 1.39 us: local(): bf.reshape(pair, 1)]
    all_to_all x2 -> x0, starting transfers between devices: 11 us -> none  [the longest x1 6.76 us: local(): lax.all_to_all(mask_wide, 'row', split_axis=1, concat_axis=0, tiled=True)]
    unnamed x23 -> x0, local copies, waits for them, and re-layouts: 4.01 us -> none
    all_to_all x5 -> x0, local copies, waits for them, and re-layouts: 3.69 us -> none  [the longest x2 2.87 us: local(): lax.all_to_all(left_wide, 'row', split_axis=1, concat_axis=0, tiled=True)]
    reduce_sum x2 -> x0, other arithmetic: 2.46 us -> none  [the longest x1 1.7 us: local(): center = element_number - jnp.mean(element_number, axis=-1, keepdims=True)]
  transfers between devices with their start and end apart: 2 -> 0, of which waited for: 0 -> 0; matrix products, arithmetic and copies ran while one was open for 5% -> 0% of each run, Pallas kernels for 0% -> 0%
where the time goes in v1:
time: 52.9 us; the launch traced here: 52.7 us
  Pallas kernels  43.9 us (83%)
  local copies, waits for them, and re-layouts  8.03 us (15%)
  other arithmetic  0.71 us (1%)
    pallas_call x1, Pallas kernels, local(): pl.pallas_call(functools.partial(exchange_kernel, n), out_shape=(jax.Shap...  22.7 us
    pallas_call x1, Pallas kernels, local(): pl.pallas_call(functools.partial(pair_kernel, seqs, res), grid=(res // bl...  21.3 us
    reshape x1, local copies, waits for them, and re-layouts, local(): bf.reshape(pair, 1)  1.39 us
    reshape x1, local copies, waits for them, and re-layouts, local(): bl.reshape(width, 1)  1.34 us
    reshape x1, local copies, waits for them, and re-layouts, local(): br.reshape(width, 1)  1.33 us

profile of v1, /device:TPU:1, one launch (start us, length us, event | category | flops | bytes accessed | tf_op | source)
XLA Modules:
  0.0 52.7 jit_solution(798072027058723364)
XLA Ops:
  0.0 1.3 %copy.21.bl_ref = f32[32,1]{1,0:T(8,128)} copy(f32[32,1]{0,1:T(1,128)} %bitcast.20) | data formatting | bytes 256 | tf_op jit(solution)/shard_map/reshape | solution.py:269
  1.3 1.3 %copy.22.br_ref = f32[32,1]{1,0:T(8,128)} copy(f32[32,1]{0,1:T(1,128)} %bitcast.21) | data formatting | bytes 256 | tf_op jit(solution)/shard_map/reshape | solution.py:271
  2.7 0.7 %convert_bitcast_fusion = (f32[80,24]{0,1:T(8,128)S(1)}, f32[24,80]{1,0:T(8,128)S(1)}) fusion(s32[24,80]{1,0:T(8,128)} %param.11), kind=kLoop, calls=%fused_computation | loop fusion | flops 1920 | bytes 23040 | tf_op jit(solution)/shard_map/transpose | solution.py:241
  3.4 0.7 %reshape.31.flat_sj_ref = f32[1,1920]{1,0:T(1,128)} reshape(f32[24,80]{1,0:T(8,128)S(1)} %get-tuple-element.14) | data formatting | bytes 15360 | tf_op jit(solution)/shard_map/reshape | solution.py:240
  4.1 0.6 %pad.4.mask_ref = f32[24,128]{1,0:T(8,128)} pad(f32[24,80]{1,0:T(8,128)S(1)} %get-tuple-element.14, f32[]{:T(128)} %constant.2.clone.1), padding=0_0x0_48 | pad | bytes 19972 | tf_op jit(solution)/shard_map/jit(_pad)/pad | solution.py:242
  4.7 0.1 copy.20
  4.7 0.7 %reshape.32.flat_is_ref = f32[1,1920]{1,0:T(1,128)} reshape(f32[80,24]{1,0:T(8,128)S(1)} %copy.20) | data formatting | bytes 15360 | tf_op jit(solution)/shard_map/reshape | solution.py:241
  5.4 1.4 %copy.25.shift_ref = f32[128,1]{1,0:T(8,128)} copy(f32[128,1]{0,1:T(1,128)} %bitcast.19) | data formatting | bytes 1024 | tf_op jit(solution)/shard_map/reshape | solution.py:304
  6.8 1.1 %copy.23 = bf16[128,32,32]{0,2,1:T(8,128)(2,1)S(1)} copy(bf16[128,32,32]{0,1,2:T(8,128)(2,1)} %bitcast.14) | data formatting | bytes 524288 | tf_op jit(solution)/shard_map/transpose | solution.py:276
  7.9 0.9 %copy.24.wt_ref = bf16[128,1024]{1,0:T(8,128)(2,1)} copy(bf16[128,1024]{0,1:T(8,128)(2,1)S(1)} %bitcast.13) | data formatting | bytes 524288 | tf_op jit(solution)/shard_map/reshape | solution.py:276
  8.7 22.7 %shard_map.100 = (bf16[4,32,1920]{2,1,0:T(8,128)(2,1)}, bf16[4,32,1920]{2,1,0:T(8,128)(2,1)}, f32[4,24,128]{2,1,0:T(8,128)}, f32[4,24,128]{2,1,0:T(8,128)}) custom-call(bf16[24,80,256]{2,1,0:T(8,128)(2,1)} %x_ref.1, f32[1,256]{1,0:T(1,128)} %bitcast.17, f32[1,256]{1,0:T(1,128)} %bitcast.18, bf16[32,256]{1,0:T(8,128)(2,1)} %bitcast.15, f32[32,1]{1,0:T(8,128)} %copy.21.bl_ref, ...), custom_call_target="tpu_custom_call" | custom-call | tf_op jit(solution)/shard_map/pallas_call | solution.py:245
  31.4 21.3 %shard_map.101 = bf16[80,80,128]{2,1,0:T(8,128)(2,1)} custom-call(bf16[4,32,1920]{2,1,0:T(8,128)(2,1)} %get-tuple-element.9.lg_ref, bf16[4,32,1920]{2,1,0:T(8,128)(2,1)} %get-tuple-element.10.rg_ref, f32[4,24,128]{2,1,0:T(8,128)} %get-tuple-element.11.ml_ref, f32[4,24,128]{2,1,0:T(8,128)} %get-tuple-element.12.mr_ref, bf16[128,1024]{1,0:T(8,128)(2,1)} %copy.24.wt_ref, ...), custom_call_target="tpu_custom_call" | custom-call | tf_op jit(solution)/shard_map/pallas_call | solution.py:283

commit v2 on v1

--- a/solution.py
+++ b/solution.py
@@ -10,6 +10,13 @@
 MESH = pl.DeviceIdType.MESH
 LANES = 128
 VMEM_LIMIT = 56 * 1024 * 1024
+
+
+def column(line):
+    size = line.shape[1]
+    down = lax.broadcasted_iota(jnp.int32, (size, size), 0)
+    across = lax.broadcasted_iota(jnp.int32, (size, size), 1)
+    return jnp.sum(jnp.where(down == across, line, 0.0), axis=1, keepdims=True)
 
 
 def exchange_kernel(
@@ -21,16 +28,19 @@
     bl_ref,
     wr_ref,
     br_ref,
-    flat_sj_ref,
-    flat_is_ref,
-    mask_ref,
+    occ_ref,
+    wf_ref,
     lg_ref,
     rg_ref,
     ml_ref,
     mr_ref,
+    wt_ref,
     norm_sj,
     norm_is,
     left_own,
+    mask_ref,
+    final_in,
+    final_mid,
     l_send,
     l_recv,
     r_send,
@@ -59,6 +69,11 @@
 
     gain = gain_ref[...]
     bias = bias_ref[...]
+    occ = occ_ref[...].astype(jnp.float32)
+    mask_ref[...] = jnp.concatenate([occ, jnp.zeros((seqs, LANES - res), jnp.float32)], axis=1)
+    flat_sj = jnp.concatenate([occ[s : s + 1] for s in range(seqs)], axis=1)
+    turned = mask_ref[...].T[:res]
+    flat_is = jnp.concatenate([turned[i : i + 1] for i in range(res)], axis=1)
 
     def normalize(s, carry):
         e = x_ref[s].astype(jnp.float32)
@@ -80,8 +95,8 @@
 
     lax.fori_loop(0, res, reorder, 0, unroll=4)
 
-    def project(src, w_ref, b_ref, flat_ref):
-        total = b_ref[...]
+    def project(src, w_ref, b_ref, flat):
+        total = column(b_ref[...])
         acc = None
         for h in range(halves):
             part = lax.dot_general(
@@ -91,9 +106,9 @@
                 preferred_element_type=jnp.float32,
             )
             acc = part if acc is None else acc + part
-        return ((acc + total) * flat_ref[...]).astype(jnp.bfloat16)
-
-    left_own[...] = project(norm_is, wl_ref, bl_ref, flat_is_ref)
+        return ((acc + total) * flat).astype(jnp.bfloat16)
+
+    left_own[...] = project(norm_is, wl_ref, bl_ref, flat_is)
 
     others = (n - 1) + n - own.astype(jnp.int32)
     pl.semaphore_wait(barrier, others)
@@ -133,7 +148,7 @@
         for copy in left_copies(0):
             copy.start()
 
-    rg_ref[row] = project(norm_sj, wr_ref, br_ref, flat_sj_ref)
+    rg_ref[row] = project(norm_sj, wr_ref, br_ref, flat_sj)
     for d in range(1, n):
         for copy in right_copies(d):
             copy.start()
@@ -144,6 +159,14 @@
     def _():
         lg_ref[row] = left_own[...]
         ml_ref[row] = mask_ref[...]
+
+    width = left_own.shape[0]
+    final_in[...] = wf_ref[...].astype(jnp.float32)
+    for q in range(width):
+        final_mid[q * width : (q + 1) * width, :] = final_in[pl.ds(q, width, stride=width), :]
+    for k in range(width * width // LANES):
+        part = slice(k * LANES, (k + 1) * LANES)
+        wt_ref[:, part] = final_mid[part, :].T.astype(jnp.bfloat16)
 
     for d in range(1, n):
         for copy in left_copies(d) + right_copies(d):
@@ -174,7 +197,7 @@
 
 
 def pair_kernel(
-    seqs, res, lg_ref, rg_ref, ml_ref, mr_ref, wt_ref, shift_ref, out_ref, stage, right, left, outer, scale
+    seqs, res, lg_ref, rg_ref, ml_ref, mr_ref, wt_ref, shift_ref, out_ref, stage, right, left, outer, scale, shift
 ):
     n, width, _ = rg_ref.shape
     block = out_ref.shape[0]
@@ -199,6 +222,7 @@
             preferred_element_type=jnp.float32,
         )
         scale[...] = 1.0 / jnp.maximum(count, 1.0)
+        shift[...] = jnp.broadcast_to(column(shift_ref[...]), shift.shape)
 
     for i in range(block):
         left[i * width : (i + 1) * width, :] = jnp.concatenate(
@@ -220,14 +244,14 @@
                 ]
         return carry
 
-    lax.fori_loop(0, width // 2, products, 0, unroll=2)
-
-    shift = shift_ref[...]
+    lax.fori_loop(0, width // 2, products, 0, unroll=True)
+
+    moved = shift[...]
     for c in range(block // 2):
         acc = jnp.dot(wt_ref[...], outer[:, c * wide : (c + 1) * wide], preferred_element_type=jnp.float32)
         for h in range(2):
             i = 2 * c + h
-            one = (acc[:, h * LANES : (h + 1) * LANES] + shift) * scale[pl.ds(step * block + i, 1), :]
+            one = (acc[:, h * LANES : (h + 1) * LANES] + moved) * scale[pl.ds(step * block + i, 1), :]
             out_ref[i] = one.T[:res].astype(jnp.bfloat16)
 
 
@@ -236,26 +260,26 @@
     width = wl.shape[1]
     pair = wf.shape[1]
     tokens = seqs * res
-    occ = occupancy.astype(jnp.float32)
-    flat_sj = occ.reshape(1, tokens)
-    flat_is = occ.T.reshape(1, tokens)
-    mask = jnp.pad(occ, ((0, 0), (0, LANES - res)))
     whole = pl.BlockSpec(memory_space=pltpu.VMEM)
     dma = pltpu.SemaphoreType.DMA((n,))
-    lg, rg, ml, mr = pl.pallas_call(
+    lg, rg, ml, mr, wt = pl.pallas_call(
         functools.partial(exchange_kernel, n),
         out_shape=(
             jax.ShapeDtypeStruct((n, width, tokens), jnp.bfloat16),
             jax.ShapeDtypeStruct((n, width, tokens), jnp.bfloat16),
             jax.ShapeDtypeStruct((n, seqs, LANES), jnp.float32),
             jax.ShapeDtypeStruct((n, seqs, LANES), jnp.float32),
+            jax.ShapeDtypeStruct((pair, width * width), jnp.bfloat16),
         ),
-        in_specs=[whole] * 10,
-        out_specs=(whole,) * 4,
+        in_specs=[whole] * 9,
+        out_specs=(whole,) * 5,
         scratch_shapes=[
             pltpu.VMEM((feat // LANES, tokens, LANES), jnp.float32),
             pltpu.VMEM((feat // LANES, tokens, LANES), jnp.float32),
             pltpu.VMEM((width, tokens), jnp.bfloat16),
+            pltpu.VMEM((seqs, LANES), jnp.float32),
+            pltpu.VMEM((width * width, pair), jnp.float32),
+            pltpu.VMEM((width * width, pair), jnp.float32),
         ]
         + [dma] * 8,
         compiler_params=pltpu.CompilerParams(
@@ -266,14 +290,12 @@
         gain.reshape(1, feat),
         bias.reshape(1, feat),
         wl.T,
-        bl.reshape(width, 1),
+        bl.reshape(1, width),
         wr.T,
-        br.reshape(width, 1),
-        flat_sj,
-        flat_is,
-        mask,
+        br.reshape(1, width),
+        occupancy,
+        wf,
     )
-    wt = jnp.transpose(wf.reshape(width, width, pair), (2, 1, 0)).reshape(pair, width * width)
     block = 16
     depth = n * seqs
 
@@ -290,7 +312,7 @@
             fixed(n, seqs, LANES),
             fixed(n, seqs, LANES),
             fixed(pair, width * width),
-            fixed(pair, 1),
+            fixed(1, pair),
         ],
         out_specs=pl.BlockSpec((block, res, pair), lambda b: (b, 0, 0)),
         scratch_shapes=[
@@ -299,9 +321,10 @@
             pltpu.VMEM((block * width, depth), jnp.bfloat16),
             pltpu.VMEM((width * width, block * LANES), jnp.bfloat16),
             pltpu.VMEM((LANES, LANES), jnp.float32),
+            pltpu.VMEM((pair, LANES), jnp.float32),
         ],
         compiler_params=pltpu.CompilerParams(vmem_limit_bytes=VMEM_LIMIT),
-    )(lg, rg, ml, mr, wt, bf.reshape(pair, 1))
+    )(lg, rg, ml, mr, wt, bf.reshape(1, pair))
 
 
 def solution(mesh):

time: 52.9 us -> 36.8 us (0.70)
  local copies, waits for them, and re-layouts: 8.03 us -> 0 us
  Pallas kernels: 43.9 us -> 36.6 us
  other arithmetic: 0.71 us -> 0 us
    pallas_call x1, Pallas kernels: 21.3 us -> 13.6 us  [local(): pl.pallas_call(functools.partial(pair_kernel, seqs, res), grid=(res // bl...]
    reshape x6 -> x0, local copies, waits for them, and re-layouts: 6.29 us -> none  [the longest x1 1.39 us: local(): bf.reshape(pair, 1)]
    transpose x2 -> x0, local copies, waits for them, and re-layouts: 1.14 us -> none  [the longest x1 1.05 us: local(): jnp.transpose(wf.reshape(width, width, pair), (2, 1, 0))]
    transpose x1 -> x0, other arithmetic: 0.71 us -> none  [local(): flat_is = occ.T.reshape(1, tokens)]
    pad x1 -> x0, local copies, waits for them, and re-layouts: 0.6 us -> none  [local(): mask = jnp.pad(occ, ((0, 0), (0, LANES - res)))]
where the time goes in v2:
time: 36.8 us; the launch traced here: 36.6 us
  Pallas kernels  36.6 us (99%)
    pallas_call x1, Pallas kernels, local(): pl.pallas_call(functools.partial(exchange_kernel, n), out_shape=(jax.Shap...  23.1 us
    pallas_call x1, Pallas kernels, local(): pl.pallas_call(functools.partial(pair_kernel, seqs, res), grid=(res // bl...  13.6 us

profile of v2, /device:TPU:1, one launch (start us, length us, event | category | flops | bytes accessed | tf_op | source)
XLA Modules:
  0.0 36.6 jit_solution(8039861791358444541)
XLA Ops:
  0.0 23.1 %shard_map.100 = (bf16[4,32,1920]{2,1,0:T(8,128)(2,1)}, bf16[4,32,1920]{2,1,0:T(8,128)(2,1)}, f32[4,24,128]{2,1,0:T(8,128)}, f32[4,24,128]{2,1,0:T(8,128)}, bf16[128,1024]{1,0:T(8,128)(2,1)}) custom-call(bf16[24,80,256]{2,1,0:T(8,128)(2,1)} %x_ref.1, f32[1,256]{1,0:T(1,128)} %bitcast.9, f32[1,256]{1,0:T(1,128)} %bitcast.10, bf16[32,256]{1,0:T(8,128)(2,1)} %bitcast.7, ...), custom_call_target="tpu_custom_call" | custom-call | tf_op jit(solution)/shard_map/pallas_call | solution.py:265
  23.1 13.6 %shard_map.101 = bf16[80,80,128]{2,1,0:T(8,128)(2,1)} custom-call(bf16[4,32,1920]{2,1,0:T(8,128)(2,1)} %get-tuple-element.10.lg_ref, bf16[4,32,1920]{2,1,0:T(8,128)(2,1)} %get-tuple-element.11.rg_ref, f32[4,24,128]{2,1,0:T(8,128)} %get-tuple-element.12.ml_ref, f32[4,24,128]{2,1,0:T(8,128)} %get-tuple-element.13.mr_ref, ...), custom_call_target="tpu_custom_call" | custom-call | tf_op jit(solution)/shard_map/pallas_call | solution.py:305

commit v3 on v2

--- a/solution.py
+++ b/solution.py
@@ -9,6 +9,7 @@
 
 MESH = pl.DeviceIdType.MESH
 LANES = 128
+GROUP = 8
 VMEM_LIMIT = 56 * 1024 * 1024
 
 
@@ -52,6 +53,8 @@
 ):
     seqs, res, feat = x_ref.shape
     halves = feat // LANES
+    groups = seqs // GROUP
+    chunk = GROUP * res
     tokens = seqs * res
     grp = lax.axis_index("grp")
     row = lax.axis_index("row")
@@ -85,7 +88,63 @@
             norm_sj[h, pl.ds(at, res), :] = v[:, h * LANES : (h + 1) * LANES]
         return carry
 
-    lax.fori_loop(0, seqs, normalize, 0)
+    def project(src, low, size, w_ref, add, flat):
+        acc = None
+        for h in range(halves):
+            part = lax.dot_general(
+                w_ref[:, h * LANES : (h + 1) * LANES],
+                src[h, low : low + size].astype(jnp.bfloat16),
+                (((1,), (1,)), ((), ())),
+                preferred_element_type=jnp.float32,
+            )
+            acc = part if acc is None else acc + part
+        return ((acc + add) * flat).astype(jnp.bfloat16)
+
+    add_left = column(bl_ref[...])
+    add_right = column(br_ref[...])
+
+    others = (n - 1) + n - own.astype(jnp.int32)
+    pl.semaphore_wait(barrier, others)
+
+    def left_copy(d):
+        return pltpu.make_async_remote_copy(
+            src_ref=left_own, dst_ref=lg_ref.at[row], send_sem=l_send.at[d], recv_sem=l_recv.at[row],
+            device_id=(grp, col, lax.rem(col + d, n)), device_id_type=MESH,
+        )
+
+    def left_mask_copy(d):
+        return pltpu.make_async_remote_copy(
+            src_ref=mask_ref, dst_ref=ml_ref.at[row], send_sem=ml_send.at[d], recv_sem=ml_recv.at[row],
+            device_id=(grp, col, lax.rem(col + d, n)), device_id_type=MESH,
+        )
+
+    def right_copy(d, g):
+        piece = rg_ref.at[row, :, pl.ds(g * chunk, chunk)]
+        return pltpu.make_async_remote_copy(
+            src_ref=piece, dst_ref=piece, send_sem=r_send.at[d, g], recv_sem=r_recv.at[row, g],
+            device_id=(grp, lax.rem(row + d, n), col), device_id_type=MESH,
+        )
+
+    def right_mask_copy(d):
+        return pltpu.make_async_remote_copy(
+            src_ref=mask_ref, dst_ref=mr_ref.at[row], send_sem=mr_send.at[d], recv_sem=mr_recv.at[row],
+            device_id=(grp, lax.rem(row + d, n), col), device_id_type=MESH,
+        )
+
+    for d in range(1, n):
+        left_mask_copy(d).start()
+        right_mask_copy(d).start()
+
+    @pl.when(jnp.logical_not(own))
+    def _():
+        left_mask_copy(0).start()
+
+    for g in range(groups):
+        lax.fori_loop(g * GROUP, (g + 1) * GROUP, normalize, 0, unroll=4)
+        part = slice(g * chunk, (g + 1) * chunk)
+        rg_ref[row, :, part] = project(norm_sj, g * chunk, chunk, wr_ref, add_right, flat_sj[:, part])
+        for d in range(1, n):
+            right_copy(d, g).start()
 
     def reorder(i, carry):
         at = pl.multiple_of(i * seqs, 8)
@@ -95,63 +154,13 @@
 
     lax.fori_loop(0, res, reorder, 0, unroll=4)
 
-    def project(src, w_ref, b_ref, flat):
-        total = column(b_ref[...])
-        acc = None
-        for h in range(halves):
-            part = lax.dot_general(
-                w_ref[:, h * LANES : (h + 1) * LANES],
-                src[h].astype(jnp.bfloat16),
-                (((1,), (1,)), ((), ())),
-                preferred_element_type=jnp.float32,
-            )
-            acc = part if acc is None else acc + part
-        return ((acc + total) * flat).astype(jnp.bfloat16)
-
-    left_own[...] = project(norm_is, wl_ref, bl_ref, flat_is)
-
-    others = (n - 1) + n - own.astype(jnp.int32)
-    pl.semaphore_wait(barrier, others)
-
-    def left_copies(d):
-        target = (grp, col, lax.rem(col + d, n))
-        return (
-            pltpu.make_async_remote_copy(
-                src_ref=left_own, dst_ref=lg_ref.at[row], send_sem=l_send.at[d], recv_sem=l_recv.at[row],
-                device_id=target, device_id_type=MESH,
-            ),
-            pltpu.make_async_remote_copy(
-                src_ref=mask_ref, dst_ref=ml_ref.at[row], send_sem=ml_send.at[d], recv_sem=ml_recv.at[row],
-                device_id=target, device_id_type=MESH,
-            ),
-        )
-
-    def right_copies(d):
-        target = (grp, lax.rem(row + d, n), col)
-        return (
-            pltpu.make_async_remote_copy(
-                src_ref=rg_ref.at[row], dst_ref=rg_ref.at[row], send_sem=r_send.at[d], recv_sem=r_recv.at[row],
-                device_id=target, device_id_type=MESH,
-            ),
-            pltpu.make_async_remote_copy(
-                src_ref=mask_ref, dst_ref=mr_ref.at[row], send_sem=mr_send.at[d], recv_sem=mr_recv.at[row],
-                device_id=target, device_id_type=MESH,
-            ),
-        )
-
-    for d in range(1, n):
-        for copy in left_copies(d):
-            copy.start()
-
-    @pl.when(jnp.logical_not(own))
-    def _():
-        for copy in left_copies(0):
-            copy.start()
-
-    rg_ref[row] = project(norm_sj, wr_ref, br_ref, flat_sj)
-    for d in range(1, n):
-        for copy in right_copies(d):
-            copy.start()
+    left_own[...] = project(norm_is, 0, tokens, wl_ref, add_left, flat_is)
+    for d in range(n - 1, 0, -1):
+        left_copy(d).start()
+
+    @pl.when(jnp.logical_not(own))
+    def _():
+        left_copy(0).start()
 
     mr_ref[row] = mask_ref[...]
 
@@ -169,31 +178,35 @@
         wt_ref[:, part] = final_mid[part, :].T.astype(jnp.bfloat16)
 
     for d in range(1, n):
-        for copy in left_copies(d) + right_copies(d):
-            copy.wait_send()
-
-    @pl.when(jnp.logical_not(own))
-    def _():
-        for copy in left_copies(0):
-            copy.wait_send()
-
-    def arrived(dst, slot, sem):
+        left_mask_copy(d).wait_send()
+        right_mask_copy(d).wait_send()
+        left_copy(d).wait_send()
+        for g in range(groups):
+            right_copy(d, g).wait_send()
+
+    @pl.when(jnp.logical_not(own))
+    def _():
+        left_mask_copy(0).wait_send()
+        left_copy(0).wait_send()
+
+    def arrived(dst, sem):
         pltpu.make_async_remote_copy(
-            src_ref=dst.at[slot], dst_ref=dst.at[slot], send_sem=l_send.at[0], recv_sem=sem.at[slot],
+            src_ref=dst, dst_ref=dst, send_sem=l_send.at[0], recv_sem=sem,
             device_id=(grp, lax.rem(row + 1, n), col), device_id_type=MESH,
         ).wait_recv()
 
     for d in range(1, n):
         slot = lax.rem(row + d, n)
-        arrived(rg_ref, slot, r_recv)
-        arrived(mr_ref, slot, mr_recv)
-        arrived(lg_ref, slot, l_recv)
-        arrived(ml_ref, slot, ml_recv)
-
-    @pl.when(jnp.logical_not(own))
-    def _():
-        arrived(lg_ref, row, l_recv)
-        arrived(ml_ref, row, ml_recv)
+        arrived(mr_ref.at[slot], mr_recv.at[slot])
+        arrived(ml_ref.at[slot], ml_recv.at[slot])
+        for g in range(groups):
+            arrived(rg_ref.at[slot, :, pl.ds(g * chunk, chunk)], r_recv.at[slot, g])
+        arrived(lg_ref.at[slot], l_recv.at[slot])
+
+    @pl.when(jnp.logical_not(own))
+    def _():
+        arrived(lg_ref.at[row], l_recv.at[row])
+        arrived(ml_ref.at[row], ml_recv.at[row])
 
 
 def pair_kernel(
@@ -281,7 +294,9 @@
             pltpu.VMEM((width * width, pair), jnp.float32),
             pltpu.VMEM((width * width, pair), jnp.float32),
         ]
-        + [dma] * 8,
+        + [dma] * 2
+        + [pltpu.SemaphoreType.DMA((n, seqs // GROUP))] * 2
+        + [dma] * 4,
         compiler_params=pltpu.CompilerParams(
             collective_id=0, has_side_effects=True, vmem_limit_bytes=VMEM_LIMIT
         ),

time: 36.8 us -> 36.5 us (level)
  the two profiles are of different devices: /device:TPU:1 before, /device:TPU:6 now
where the time goes in v3:
time: 36.5 us; the launch traced here: 36.4 us
  Pallas kernels  36.4 us (100%)
    pallas_call x1, Pallas kernels, local(): pl.pallas_call(functools.partial(exchange_kernel, n), out_shape=(jax.Shap...  22.8 us
    pallas_call x1, Pallas kernels, local(): pl.pallas_call(functools.partial(pair_kernel, seqs, res), grid=(res // bl...  13.6 us

profile of v3, /device:TPU:6, one launch (start us, length us, event | category | flops | bytes accessed | tf_op | source)
XLA Modules:
  0.0 36.4 jit_solution(5153124592353910291)
XLA Ops:
  0.0 22.8 %shard_map.100 = (bf16[4,32,1920]{2,1,0:T(8,128)(2,1)}, bf16[4,32,1920]{2,1,0:T(8,128)(2,1)}, f32[4,24,128]{2,1,0:T(8,128)}, f32[4,24,128]{2,1,0:T(8,128)}, bf16[128,1024]{1,0:T(8,128)(2,1)}) custom-call(bf16[24,80,256]{2,1,0:T(8,128)(2,1)} %x_ref.1, f32[1,256]{1,0:T(1,128)} %bitcast.9, f32[1,256]{1,0:T(1,128)} %bitcast.10, bf16[32,256]{1,0:T(8,128)(2,1)} %bitcast.7, ...), custom_call_target="tpu_custom_call" | custom-call | tf_op jit(solution)/shard_map/pallas_call | solution.py:278
  22.8 13.6 %shard_map.101 = bf16[80,80,128]{2,1,0:T(8,128)(2,1)} custom-call(bf16[4,32,1920]{2,1,0:T(8,128)(2,1)} %get-tuple-element.10.lg_ref, bf16[4,32,1920]{2,1,0:T(8,128)(2,1)} %get-tuple-element.11.rg_ref, f32[4,24,128]{2,1,0:T(8,128)} %get-tuple-element.12.ml_ref, f32[4,24,128]{2,1,0:T(8,128)} %get-tuple-element.13.mr_ref, ...), custom_call_target="tpu_custom_call" | custom-call | tf_op jit(solution)/shard_map/pallas_call | solution.py:320

commit v4 on v3

--- a/solution.py
+++ b/solution.py
@@ -38,10 +38,12 @@
     wt_ref,
     norm_sj,
     norm_is,
-    left_own,
+    line,
     mask_ref,
     final_in,
     final_mid,
+    z_send,
+    z_recv,
     l_send,
     l_recv,
     r_send,
@@ -70,6 +72,15 @@
     def _():
         pl.semaphore_signal(barrier, inc=1, device_id=(grp, row, row), device_id_type=MESH)
 
+    def inside(place):
+        return jnp.logical_and(place >= 0, place < n)
+
+    for way in (-1, 1):
+
+        @pl.when(inside(col + way))
+        def _():
+            pl.semaphore_signal(barrier, inc=1, device_id=(grp, row, col + way), device_id_type=MESH)
+
     gain = gain_ref[...]
     bias = bias_ref[...]
     occ = occ_ref[...].astype(jnp.float32)
@@ -103,13 +114,19 @@
     add_left = column(bl_ref[...])
     add_right = column(br_ref[...])
 
-    others = (n - 1) + n - own.astype(jnp.int32)
+    others = (n - 1) + n - own.astype(jnp.int32) + (col > 0).astype(jnp.int32) + (col < n - 1).astype(jnp.int32)
     pl.semaphore_wait(barrier, others)
 
-    def left_copy(d):
+    def hop_copy(src, way):
         return pltpu.make_async_remote_copy(
-            src_ref=left_own, dst_ref=lg_ref.at[row], send_sem=l_send.at[d], recv_sem=l_recv.at[row],
-            device_id=(grp, col, lax.rem(col + d, n)), device_id_type=MESH,
+            src_ref=line.at[src], dst_ref=line.at[src], send_sem=z_send.at[(way + 1) // 2, src], recv_sem=z_recv.at[src],
+            device_id=(grp, row, col + way), device_id_type=MESH,
+        )
+
+    def left_copy(src):
+        return pltpu.make_async_remote_copy(
+            src_ref=line.at[src], dst_ref=lg_ref.at[row], send_sem=l_send.at[src], recv_sem=l_recv.at[row],
+            device_id=(grp, src, col), device_id_type=MESH,
         )
 
     def left_mask_copy(d):
@@ -154,22 +171,25 @@
 
     lax.fori_loop(0, res, reorder, 0, unroll=4)
 
-    left_own[...] = project(norm_is, 0, tokens, wl_ref, add_left, flat_is)
-    for d in range(n - 1, 0, -1):
-        left_copy(d).start()
+    line[col] = project(norm_is, 0, tokens, wl_ref, add_left, flat_is)
+    for way in (-1, 1):
+
+        @pl.when(inside(col + way))
+        def _():
+            hop_copy(col, way).start()
 
     @pl.when(jnp.logical_not(own))
     def _():
-        left_copy(0).start()
+        left_copy(col).start()
 
     mr_ref[row] = mask_ref[...]
 
     @pl.when(own)
     def _():
-        lg_ref[row] = left_own[...]
+        lg_ref[row] = line[col]
         ml_ref[row] = mask_ref[...]
 
-    width = left_own.shape[0]
+    width = line.shape[1]
     final_in[...] = wf_ref[...].astype(jnp.float32)
     for q in range(width):
         final_mid[q * width : (q + 1) * width, :] = final_in[pl.ds(q, width, stride=width), :]
@@ -177,23 +197,60 @@
         part = slice(k * LANES, (k + 1) * LANES)
         wt_ref[:, part] = final_mid[part, :].T.astype(jnp.bfloat16)
 
-    for d in range(1, n):
-        left_mask_copy(d).wait_send()
-        right_mask_copy(d).wait_send()
-        left_copy(d).wait_send()
-        for g in range(groups):
-            right_copy(d, g).wait_send()
-
-    @pl.when(jnp.logical_not(own))
-    def _():
-        left_mask_copy(0).wait_send()
-        left_copy(0).wait_send()
-
     def arrived(dst, sem):
         pltpu.make_async_remote_copy(
             src_ref=dst, dst_ref=dst, send_sem=l_send.at[0], recv_sem=sem,
             device_id=(grp, lax.rem(row + 1, n), col), device_id_type=MESH,
         ).wait_recv()
+
+    for h in range(1, n):
+        for way in (-1, 1):
+            src = col - way * h
+
+            @pl.when(inside(src))
+            def _():
+                arrived(line.at[src], z_recv.at[src])
+
+                @pl.when(inside(col + way))
+                def _():
+                    hop_copy(src, way).start()
+
+                @pl.when(src != row)
+                def _():
+                    left_copy(src).start()
+
+                @pl.when(src == row)
+                def _():
+                    lg_ref[row] = line[src]
+
+    for h in range(1, n):
+        for way in (-1, 1):
+            src = col - way * h
+
+            @pl.when(jnp.logical_and(inside(src), inside(col + way)))
+            def _():
+                hop_copy(src, way).wait_send()
+
+            @pl.when(jnp.logical_and(inside(src), src != row))
+            def _():
+                left_copy(src).wait_send()
+
+    for way in (-1, 1):
+
+        @pl.when(inside(col + way))
+        def _():
+            hop_copy(col, way).wait_send()
+
+    for d in range(1, n):
+        left_mask_copy(d).wait_send()
+        right_mask_copy(d).wait_send()
+        for g in range(groups):
+            right_copy(d, g).wait_send()
+
+    @pl.when(jnp.logical_not(own))
+    def _():
+        left_mask_copy(0).wait_send()
+        left_copy(col).wait_send()
 
     for d in range(1, n):
         slot = lax.rem(row + d, n)
@@ -205,7 +262,6 @@
 
     @pl.when(jnp.logical_not(own))
     def _():
-        arrived(lg_ref.at[row], l_recv.at[row])
         arrived(ml_ref.at[row], ml_recv.at[row])
 
 
@@ -289,11 +345,12 @@
         scratch_shapes=[
             pltpu.VMEM((feat // LANES, tokens, LANES), jnp.float32),
             pltpu.VMEM((feat // LANES, tokens, LANES), jnp.float32),
-            pltpu.VMEM((width, tokens), jnp.bfloat16),
+            pltpu.VMEM((n, width, tokens), jnp.bfloat16),
             pltpu.VMEM((seqs, LANES), jnp.float32),
             pltpu.VMEM((width * width, pair), jnp.float32),
             pltpu.VMEM((width * width, pair), jnp.float32),
         ]
+        + [pltpu.SemaphoreType.DMA((2, n)), dma]
         + [dma] * 2
         + [pltpu.SemaphoreType.DMA((n, seqs // GROUP))] * 2
         + [dma] * 4,

time: 36.5 us -> 39.8 us (1.090)
  the two profiles are of different devices: /device:TPU:6 before, /device:TPU:0 now
where the time goes in v4:
time: 39.8 us; the launch traced here: 39.6 us
  Pallas kernels  39.6 us (99%)
    pallas_call x1, Pallas kernels, local(): pl.pallas_call(functools.partial(exchange_kernel, n), out_shape=(jax.Shap...  26 us
    pallas_call x1, Pallas kernels, local(): pl.pallas_call(functools.partial(pair_kernel, seqs, res), grid=(res // bl...  13.6 us

profile of v4, /device:TPU:0, one launch (start us, length us, event | category | flops | bytes accessed | tf_op | source)
XLA Modules:
  0.0 39.6 jit_solution(3534950993807839816)
XLA Ops:
  0.0 26.0 %shard_map.100 = (bf16[4,32,1920]{2,1,0:T(8,128)(2,1)}, bf16[4,32,1920]{2,1,0:T(8,128)(2,1)}, f32[4,24,128]{2,1,0:T(8,128)}, f32[4,24,128]{2,1,0:T(8,128)}, bf16[128,1024]{1,0:T(8,128)(2,1)}) custom-call(bf16[24,80,256]{2,1,0:T(8,128)(2,1)} %x_ref.1, f32[1,256]{1,0:T(1,128)} %bitcast.9, f32[1,256]{1,0:T(1,128)} %bitcast.10, bf16[32,256]{1,0:T(8,128)(2,1)} %bitcast.7, ...), custom_call_target="tpu_custom_call" | custom-call | tf_op jit(solution)/shard_map/pallas_call | solution.py:334
  26.0 13.6 %shard_map.101 = bf16[80,80,128]{2,1,0:T(8,128)(2,1)} custom-call(bf16[4,32,1920]{2,1,0:T(8,128)(2,1)} %get-tuple-element.10.lg_ref, bf16[4,32,1920]{2,1,0:T(8,128)(2,1)} %get-tuple-element.11.rg_ref, f32[4,24,128]{2,1,0:T(8,128)} %get-tuple-element.12.ml_ref, f32[4,24,128]{2,1,0:T(8,128)} %get-tuple-element.13.mr_ref, ...), custom_call_target="tpu_custom_call" | custom-call | tf_op jit(solution)/shard_map/pallas_call | solution.py:377

commit v5 on v3

--- a/solution.py
+++ b/solution.py
@@ -46,6 +46,7 @@
     l_recv,
     r_send,
     r_recv,
+    s_send,
     ml_send,
     ml_recv,
     mr_send,
@@ -60,6 +61,7 @@
     row = lax.axis_index("row")
     col = lax.axis_index("col")
     own = row == col
+    sibling = row + 1 - 2 * lax.rem(row, 2)
 
     barrier = pltpu.get_barrier_semaphore()
     for d in range(1, n):
@@ -125,6 +127,20 @@
             device_id=(grp, lax.rem(row + d, n), col), device_id_type=MESH,
         )
 
+    def sibling_copy(j, g):
+        slot = lax.rem(row + 2 * j, n)
+        piece = rg_ref.at[slot, :, pl.ds(g * chunk, chunk)]
+        return pltpu.make_async_remote_copy(
+            src_ref=piece, dst_ref=piece, send_sem=s_send.at[j, g], recv_sem=r_recv.at[slot, g],
+            device_id=(grp, sibling, col), device_id_type=MESH,
+        )
+
+    def arrived(dst, sem):
+        pltpu.make_async_remote_copy(
+            src_ref=dst, dst_ref=dst, send_sem=l_send.at[0], recv_sem=sem,
+            device_id=(grp, sibling, col), device_id_type=MESH,
+        ).wait_recv()
+
     def right_mask_copy(d):
         return pltpu.make_async_remote_copy(
             src_ref=mask_ref, dst_ref=mr_ref.at[row], send_sem=mr_send.at[d], recv_sem=mr_recv.at[row],
@@ -143,8 +159,9 @@
         lax.fori_loop(g * GROUP, (g + 1) * GROUP, normalize, 0, unroll=4)
         part = slice(g * chunk, (g + 1) * chunk)
         rg_ref[row, :, part] = project(norm_sj, g * chunk, chunk, wr_ref, add_right, flat_sj[:, part])
-        for d in range(1, n):
+        for d in range(2, n, 2):
             right_copy(d, g).start()
+        sibling_copy(0, g).start()
 
     def reorder(i, carry):
         at = pl.multiple_of(i * seqs, 8)
@@ -161,6 +178,12 @@
     @pl.when(jnp.logical_not(own))
     def _():
         left_copy(0).start()
+
+    for g in range(groups):
+        for j in range(1, n // 2):
+            slot = lax.rem(row + 2 * j, n)
+            arrived(rg_ref.at[slot, :, pl.ds(g * chunk, chunk)], r_recv.at[slot, g])
+            sibling_copy(j, g).start()
 
     mr_ref[row] = mask_ref[...]
 
@@ -177,30 +200,29 @@
         part = slice(k * LANES, (k + 1) * LANES)
         wt_ref[:, part] = final_mid[part, :].T.astype(jnp.bfloat16)
 
+    for g in range(groups):
+        for d in range(2, n, 2):
+            right_copy(d, g).wait_send()
+        for j in range(n // 2):
+            sibling_copy(j, g).wait_send()
     for d in range(1, n):
         left_mask_copy(d).wait_send()
         right_mask_copy(d).wait_send()
         left_copy(d).wait_send()
-        for g in range(groups):
-            right_copy(d, g).wait_send()
 
     @pl.when(jnp.logical_not(own))
     def _():
         left_mask_copy(0).wait_send()
         left_copy(0).wait_send()
 
-    def arrived(dst, sem):
-        pltpu.make_async_remote_copy(
-            src_ref=dst, dst_ref=dst, send_sem=l_send.at[0], recv_sem=sem,
-            device_id=(grp, lax.rem(row + 1, n), col), device_id_type=MESH,
-        ).wait_recv()
-
+    for g in range(groups):
+        for j in range(n // 2):
+            slot = lax.rem(sibling + 2 * j, n)
+            arrived(rg_ref.at[slot, :, pl.ds(g * chunk, chunk)], r_recv.at[slot, g])
     for d in range(1, n):
         slot = lax.rem(row + d, n)
         arrived(mr_ref.at[slot], mr_recv.at[slot])
         arrived(ml_ref.at[slot], ml_recv.at[slot])
-        for g in range(groups):
-            arrived(rg_ref.at[slot, :, pl.ds(g * chunk, chunk)], r_recv.at[slot, g])
         arrived(lg_ref.at[slot], l_recv.at[slot])
 
     @pl.when(jnp.logical_not(own))
@@ -295,7 +317,7 @@
             pltpu.VMEM((width * width, pair), jnp.float32),
         ]
         + [dma] * 2
-        + [pltpu.SemaphoreType.DMA((n, seqs // GROUP))] * 2
+        + [pltpu.SemaphoreType.DMA((n, seqs // GROUP))] * 3
         + [dma] * 4,
         compiler_params=pltpu.CompilerParams(
             collective_id=0, has_side_effects=True, vmem_limit_bytes=VMEM_LIMIT

time: 36.5 us -> 36.6 us (level)
  the two profiles are of different devices: /device:TPU:6 before, /device:TPU:2 now
where the time goes in v5:
time: 36.6 us; the launch traced here: 36.4 us
  Pallas kernels  36.4 us (99%)
    pallas_call x1, Pallas kernels, local(): pl.pallas_call(functools.partial(exchange_kernel, n), out_shape=(jax.Shap...  22.8 us
    pallas_call x1, Pallas kernels, local(): pl.pallas_call(functools.partial(pair_kernel, seqs, res), grid=(res // bl...  13.6 us

profile of v5, /device:TPU:2, one launch (start us, length us, event | category | flops | bytes accessed | tf_op | source)
XLA Modules:
  0.0 36.4 jit_solution(11552801719784455333)
XLA Ops:
  0.0 22.8 %shard_map.100 = (bf16[4,32,1920]{2,1,0:T(8,128)(2,1)}, bf16[4,32,1920]{2,1,0:T(8,128)(2,1)}, f32[4,24,128]{2,1,0:T(8,128)}, f32[4,24,128]{2,1,0:T(8,128)}, bf16[128,1024]{1,0:T(8,128)(2,1)}) custom-call(bf16[24,80,256]{2,1,0:T(8,128)(2,1)} %x_ref.1, f32[1,256]{1,0:T(1,128)} %bitcast.9, f32[1,256]{1,0:T(1,128)} %bitcast.10, bf16[32,256]{1,0:T(8,128)(2,1)} %bitcast.7, ...), custom_call_target="tpu_custom_call" | custom-call | tf_op jit(solution)/shard_map/pallas_call | solution.py:300
  22.9 13.6 %shard_map.101 = bf16[80,80,128]{2,1,0:T(8,128)(2,1)} custom-call(bf16[4,32,1920]{2,1,0:T(8,128)(2,1)} %get-tuple-element.10.lg_ref, bf16[4,32,1920]{2,1,0:T(8,128)(2,1)} %get-tuple-element.11.rg_ref, f32[4,24,128]{2,1,0:T(8,128)} %get-tuple-element.12.ml_ref, f32[4,24,128]{2,1,0:T(8,128)} %get-tuple-element.13.mr_ref, ...), custom_call_target="tpu_custom_call" | custom-call | tf_op jit(solution)/shard_map/pallas_call | solution.py:342

commit v6 on v2

--- a/solution.py
+++ b/solution.py
@@ -85,7 +85,7 @@
             norm_sj[h, pl.ds(at, res), :] = v[:, h * LANES : (h + 1) * LANES]
         return carry
 
-    lax.fori_loop(0, seqs, normalize, 0)
+    lax.fori_loop(0, seqs, normalize, 0, unroll=4)
 
     def reorder(i, carry):
         at = pl.multiple_of(i * seqs, 8)

time: 36.8 us -> 34.7 us (0.943)
  Pallas kernels: 36.6 us -> 34.6 us
    pallas_call x1, Pallas kernels: 23.1 us -> 21 us  [local(): pl.pallas_call(functools.partial(exchange_kernel, n), out_shape=(jax.Shap...]
where the time goes in v6:
time: 34.7 us; the launch traced here: 34.6 us
  Pallas kernels  34.6 us (100%)
    pallas_call x1, Pallas kernels, local(): pl.pallas_call(functools.partial(exchange_kernel, n), out_shape=(jax.Shap...  21 us
    pallas_call x1, Pallas kernels, local(): pl.pallas_call(functools.partial(pair_kernel, seqs, res), grid=(res // bl...  13.6 us

profile of v6, /device:TPU:1, one launch (start us, length us, event | category | flops | bytes accessed | tf_op | source)
XLA Modules:
  0.0 34.6 jit_solution(14501016887247656704)
XLA Ops:
  0.0 21.0 %shard_map.100 = (bf16[4,32,1920]{2,1,0:T(8,128)(2,1)}, bf16[4,32,1920]{2,1,0:T(8,128)(2,1)}, f32[4,24,128]{2,1,0:T(8,128)}, f32[4,24,128]{2,1,0:T(8,128)}, bf16[128,1024]{1,0:T(8,128)(2,1)}) custom-call(bf16[24,80,256]{2,1,0:T(8,128)(2,1)} %x_ref.1, f32[1,256]{1,0:T(1,128)} %bitcast.9, f32[1,256]{1,0:T(1,128)} %bitcast.10, bf16[32,256]{1,0:T(8,128)(2,1)} %bitcast.7, ...), custom_call_target="tpu_custom_call" | custom-call | tf_op jit(solution)/shard_map/pallas_call | solution.py:265
  21.0 13.6 %shard_map.101 = bf16[80,80,128]{2,1,0:T(8,128)(2,1)} custom-call(bf16[4,32,1920]{2,1,0:T(8,128)(2,1)} %get-tuple-element.10.lg_ref, bf16[4,32,1920]{2,1,0:T(8,128)(2,1)} %get-tuple-element.11.rg_ref, f32[4,24,128]{2,1,0:T(8,128)} %get-tuple-element.12.ml_ref, f32[4,24,128]{2,1,0:T(8,128)} %get-tuple-element.13.mr_ref, ...), custom_call_target="tpu_custom_call" | custom-call | tf_op jit(solution)/shard_map/pallas_call | solution.py:305
